TPU v7x, 32 devices: a whole 2x2x4 slice. The times are simulated.
32 devices in a mesh: groups: 2 (over y), ctx: 4 (over z), dp: 2 (over x), mp: 2 (over core).
Axes of the slice: x: 2, y: 2, z: 4, core: 2. Of those that a mesh axis runs over, the one named last changes fastest.
Arguments:
- head_inputs: bfloat16 [3, 4, 1024, 1536], P(None, ('groups', 'dp'), 'ctx', 'mp'), parts along dimension 1, may hold values from -0.29882812 to 0.29882812
- write_read: bfloat16 [3, 4, 1024, 128], P(None, ('groups', 'dp'), 'ctx'), parts along dimension 1, may hold values from -0.26953125 to 0.26953125
- decay_steps: int32 [3, 4, 12, 1024], P(None, ('groups', 'dp'), 'mp', 'ctx'), parts along dimension 1, may hold values from 0 to 512
- scan_orders: int32 [2, 4, 1024], P(None, ('groups', 'dp'), 'ctx'), parts along dimension 1, may hold values from 0 to 1023, as said below
- cotangent: bfloat16 [4, 1024, 768], P(('groups', 'dp'), 'ctx'), parts along dimension 0, may hold values from -0.59765625 to 0.59765625
- out_weight: bfloat16 [3, 768, 1536], P(None, 'ctx', 'mp'), may hold values from -0.4375 to 0.4375
Outputs:
- grad_inputs: bfloat16 [3, 4, 1024, 1536], P(None, ('groups', 'dp'), 'ctx', 'mp'), parts along dimension 1
- grad_write_read: bfloat16 [3, 4, 1024, 128], P(None, ('groups', 'dp'), 'ctx'), parts along dimension 1
- grad_weight: bfloat16 [6, 768, 1536], P('groups', 'ctx', 'mp'), parts along dimension 0
There are 2 independent parts, one for each index of `groups`. A program takes and returns all parts, laid end to end along the dimension named above; an argument that names none is the same for every part. Nothing has to cross between parts.
Inputs may be any that keep to these rules, and one draw needn't show every extreme that they name: `scan_orders`: for every volume and each of the two orders, position d * 256 + q * 64 + m (0 <= m < 64) holds a patch of index q * 256 + d * 64 + m' with 0 <= m' < 64; every patch stands at exactly one position.
All inputs are finite; a program needn't handle non-finite values.
Results may differ from a plain program's by a relative error of at most 0.005.
Values may be sent and summed in bfloat16 or wider, within the bound.
A program may use at most 128 MiB of HBM per device.

v0:
```python
import math

import jax
import jax.numpy as jnp
from jax import lax
from jax.sharding import PartitionSpec as P

P_SIZE = 128
N = 64


EXACT = lax.Precision.HIGHEST


def prefix(value, axis, join, neutral, backward):
    count, mine = (lax.axis_size(axis), lax.axis_index(axis))
    pieces = jax.tree.map(lambda part: lax.all_gather(part, axis), value)
    if backward:
        pieces = jax.tree.map(lambda part: part[::-1], pieces)
        mine = count - 1 - mine
    running = jax.tree.map(
        lambda part, zero: jnp.full_like(part, 0) + jnp.asarray(zero, part.dtype), value, neutral
    )

    def lap(position, running):
        longer = join(running, jax.tree.map(lambda part: part[position], pieces))
        return jax.tree.map(lambda new, old: jnp.where(position < mine, new, old), longer, running)

    return lax.fori_loop(0, count - 1, lap, running)


def contract(form, *operands):
    return jnp.einsum(form, *operands, precision=EXACT)


def segment_parts(log_rates, writes, readers):
    running = jnp.cumsum(log_rates, axis=-1)
    final_log = running[..., -1]
    length = log_rates.shape[-1]
    causal = jnp.arange(length)[:, None] >= jnp.arange(length)[None, :]
    differ = jnp.where(causal, running[..., :, None] - running[..., None, :], 0.0)
    decay_mat = jnp.where(causal, jnp.exp(differ), 0.0)
    scores = contract("ovin,ovjn->ovij", readers, writes)
    mixing = scores[:, :, None] * decay_mat
    return (running, final_log, decay_mat, mixing)


def segment_forward(pieces, signal, writes, readers, memory):
    running, final_log, decay_mat, mixing = pieces
    rising = jnp.exp(running)
    falling = jnp.exp(final_log[..., None] - running)
    outputs = contract("ovhij,ovjhp->ovihp", mixing, signal) + contract(
        "ovhi,ovin,ovhnp->ovihp", rising, readers, memory
    )
    memory_next = jnp.exp(final_log)[..., None, None] * memory + contract(
        "ovhj,ovjn,ovjhp->ovhnp", falling, writes, signal
    )
    return (outputs, memory_next)


def segment_backward(pieces, signal, writes, readers, upstream, memory, memory_grad):
    running, final_log, decay_mat, mixing = pieces
    rising = jnp.exp(running)
    falling = jnp.exp(final_log[..., None] - running)
    grad_signal = contract("ovhij,ovihp->ovjhp", mixing, upstream) + contract(
        "ovhj,ovjn,ovhnp->ovjhp", falling, writes, memory_grad
    )
    weighted = contract("ovihp,ovjhp->ovhij", upstream, signal) * decay_mat
    grad_writes = contract("ovhij,ovin->ovjn", weighted, readers) + contract(
        "ovhj,ovjhp,ovhnp->ovjn", falling, signal, memory_grad
    )
    grad_readers = contract("ovhij,ovjn->ovin", weighted, writes) + contract(
        "ovhi,ovihp,ovhnp->ovin", rising, upstream, memory
    )
    grad_prev = jnp.exp(final_log)[..., None, None] * memory_grad + contract(
        "ovhi,ovin,ovihp->ovhnp", rising, readers, upstream
    )
    return (grad_signal, grad_writes, grad_readers, grad_prev)


def run_segments(signal, writes, readers, log_rates, upstream, memory_in, grad_in, length):
    blocks = signal.shape[2] // length

    def cut_rows(array, number, along):
        start_row = (number * length).astype(jnp.int32)
        return lax.dynamic_slice_in_dim(array, start_row, length, along)

    def forward_turn(number, carried):
        memory, outputs, memories = carried
        sig = cut_rows(signal, number, 2)
        wri = cut_rows(writes, number, 2)
        rea = cut_rows(readers, number, 2)
        pieces = segment_parts(cut_rows(log_rates, number, 3), wri, rea)
        out_rows, memory_next = segment_forward(pieces, sig, wri, rea, memory)
        outputs = lax.dynamic_update_slice_in_dim(
            outputs, out_rows, (number * length).astype(jnp.int32), 2
        )
        memories = lax.dynamic_update_index_in_dim(memories, memory, number, 0)
        return (memory_next, outputs, memories)

    start_memories = jnp.zeros((blocks,) + memory_in.shape, memory_in.dtype)
    _, outputs, memories = lax.fori_loop(
        0, blocks, forward_turn, (memory_in, jnp.zeros_like(signal), start_memories)
    )

    def backward_turn(countdown, carried):
        memory_grad, grad_signal, grad_writes, grad_readers = carried
        number = blocks - 1 - countdown
        sig = cut_rows(signal, number, 2)
        wri = cut_rows(writes, number, 2)
        rea = cut_rows(readers, number, 2)
        pieces = segment_parts(cut_rows(log_rates, number, 3), wri, rea)
        memory = lax.dynamic_index_in_dim(memories, number, 0, keepdims=False)
        part_sig, part_wri, part_rea, grad_prev = segment_backward(
            pieces, sig, wri, rea, cut_rows(upstream, number, 2), memory, memory_grad
        )
        start_row = (number * length).astype(jnp.int32)
        grad_signal = lax.dynamic_update_slice_in_dim(grad_signal, part_sig, start_row, 2)
        grad_writes = lax.dynamic_update_slice_in_dim(grad_writes, part_wri, start_row, 2)
        grad_readers = lax.dynamic_update_slice_in_dim(grad_readers, part_rea, start_row, 2)
        return (grad_prev, grad_signal, grad_writes, grad_readers)

    _, grad_signal, grad_writes, grad_readers = lax.fori_loop(
        0,
        blocks,
        backward_turn,
        (grad_in, jnp.zeros_like(signal), jnp.zeros_like(writes), jnp.zeros_like(readers)),
    )
    return (outputs, grad_signal, grad_writes, grad_readers)


def carry_forward(earlier, later):
    return (earlier[0] + later[0], jnp.exp(later[0])[..., None, None] * earlier[1] + later[1])


def carry_backward(earlier, later):
    return (earlier[0] + later[0], later[1] + jnp.exp(later[0])[..., None, None] * earlier[1])


def shards(head_inputs, write_read, decay_steps, scan_orders, cotangent, out_weight):
    volumes, tokens, model_width = cotangent.shape
    ctx_count = lax.axis_size("ctx")
    seq_len = tokens * ctx_count
    local_heads = decay_steps.shape[2]
    inner_width = head_inputs.shape[3]
    gathered = lax.all_gather(cotangent, "ctx", axis=1, tiled=True)

    def reorder(ordering):
        return jax.vmap(lambda table_rows, row_ids: table_rows[row_ids])(gathered, ordering)

    scanned = jnp.stack([cotangent, reorder(scan_orders[0]), reorder(scan_orders[1])])
    upstream = jnp.einsum(
        "ovtd,odi->ovti",
        scanned,
        lax.all_gather(out_weight, "ctx", axis=1, tiled=True),
        preferred_element_type=jnp.float32,
    ).astype(jnp.bfloat16)
    upstream = lax.optimization_barrier(upstream)
    signal = head_inputs.astype(jnp.float32).reshape(3, volumes, tokens, local_heads, P_SIZE)
    grad_up = upstream.astype(jnp.float32).reshape(3, volumes, tokens, local_heads, P_SIZE)
    writes = write_read[..., :N].astype(jnp.float32)
    readers = write_read[..., N:].astype(jnp.float32)
    log_rates = -decay_steps.astype(jnp.float32) / seq_len
    running = jnp.cumsum(log_rates, axis=-1)
    summed_log = running[..., -1]
    end_state = contract(
        "ovht,ovtn,ovthp->ovhnp", jnp.exp(summed_log[..., None] - running), writes, signal
    )
    start_grad = contract("ovht,ovtn,ovthp->ovhnp", jnp.exp(running), readers, grad_up)
    zeros_log = jnp.zeros_like(summed_log)
    zeros_state = jnp.zeros_like(end_state)
    _, state_in = prefix(
        (summed_log, end_state), "ctx", carry_forward, (zeros_log, zeros_state), False
    )
    _, grad_out = prefix(
        (summed_log, start_grad), "ctx", carry_backward, (zeros_log, zeros_state), True
    )
    length = math.gcd(tokens, 128)
    outputs, grad_signal, grad_writes, grad_readers = run_segments(
        signal, writes, readers, log_rates, grad_up, state_in, grad_out, length
    )
    grad_wr = lax.psum(jnp.concatenate([grad_writes, grad_readers], axis=-1), "mp").astype(
        jnp.bfloat16
    )
    grad_inputs = grad_signal.reshape(3, volumes, tokens, inner_width).astype(jnp.bfloat16)
    outputs_bf = outputs.reshape(3, volumes, tokens, inner_width).astype(jnp.bfloat16)
    weight_term = jnp.einsum(
        "ovtd,ovti->odi", scanned, outputs_bf, preferred_element_type=jnp.float32
    )
    rows_sum = lax.psum_scatter(weight_term, "ctx", scatter_dimension=1, tiled=True)
    weight_grad = lax.psum(rows_sum, "dp").astype(jnp.bfloat16)
    return (grad_inputs, grad_wr, weight_grad)


def solution(mesh):
    in_specs = (
        P(None, ("groups", "dp"), "ctx", "mp"),
        P(None, ("groups", "dp"), "ctx", None),
        P(None, ("groups", "dp"), "mp", "ctx"),
        P(None, ("groups", "dp"), "ctx"),
        P(("groups", "dp"), "ctx", None),
        P(None, "ctx", "mp"),
    )
    out_specs = (
        P(None, ("groups", "dp"), "ctx", "mp"),
        P(None, ("groups", "dp"), "ctx", None),
        P("groups", "ctx", "mp"),
    )
    return jax.shard_map(shards, mesh=mesh, in_specs=in_specs, out_specs=out_specs, check_vma=False)
```

profile of v0, /device:TPU:0, one launch (start us, length us, event | category | flops | bytes accessed | tf_op | source)
XLA Modules:
  0.0 406.5 jit_solution(13065868097995965039)
XLA Ops:
  8.0 0.7 fusion.84
  8.7 5.4 %reduce-window.6 = f32[3,1,6,2,128]{4,3,2,1,0:T(2,128)S(1)} reduce-window(f32[3,1,6,2,128]{4,3,2,1,0:T(2,128)S(1)} %bitcast.295, f32[]{:T(128)} %constant.173.clone.1), window={size=1x1x1x1x128 pad=0_0x0_0x0_0x0_0x127_0}, to_apply=%region_0.0 | reduce-window | flops 585216 | bytes 36868 | tf_op jit(solution)/shard_map/reduce-window
  14.6 1.1 fusion.94
  17.6 0.8 convert_bitcast_fusion.1
  18.4 2.2 fusion.72
  21.5 1.7 copy.120
  23.2 14.1 %all-gather.1 = f32[12,1,6,1]{2,3,1,0:T(1,128)} all-gather(f32[3,1,6,1]{2,3,1,0:T(1,128)S(1)} %copy.107), channel_id=3, replica_groups=mesh['groups'=2,'ctx'=4,'dp'=2,'mp'=2] {'ctx'}, dimensions={0}, use_global_device_ids=true | all-gather | bytes 360 | tf_op jit(solution)/shard_map/all_gather | solution.py:17
  37.3 12.2 %all-gather.8.cloned.1.call-done = bf16[1,1024,768]{2,1,0:T(8,128)(2,1)} async-done(((bf16[1,256,768]{2,1,0:T(8,128)(2,1)}), bf16[1,1024,768]{2,1,0:T(8,128)(2,1)}) %all-gather.8.cloned.1.call-update) | async-done | bytes 1572880 | tf_op jit(solution)/shard_map/all_gather | solution.py:146
  49.6 3.6 gather_fusion
  53.2 2.9 gather_fusion.1
  56.1 45.0 %all-gather.14.cloned.1.call-done = f32[12,6,64,128]{3,2,1,0:T(8,128)} async-done(((f32[3,6,64,128]{3,2,1,0:T(8,128)}), f32[12,6,64,128]{3,2,1,0:T(8,128)}) %all-gather.14.cloned.1.call-update) | async-done | bytes 2359312 | tf_op jit(solution)/shard_map/all_gather | solution.py:17
  101.1 5.7 %while.69 = (s32[]{:T(128)}, f32[3,1,6,64,128]{4,3,2,1,0:T(8,128)S(1)}, s32[]{:T(128)}, f32[4,3,1,6]{3,2,1,0:T(1,128)}, f32[4,3,1,6,64,128]{5,4,3,1,2,0:T(8,128)}, /*index=5*/s32[]{:T(128)}, s32[]{:T(128)}) while((s32[]{:T(128)}, f32[3,1,6,64,128]{4,3,2,1,0:T(8,128)S(1)}, s32[]{:T(128)}, f32[4,3,1,6]{3,2,1,0:T(1,128)}, ...), condition=%wide.region_5.6_spmd.clone, body=%wide.region_4.5_spmd.clone.sunk | while | flops 589828 | bytes 1769937 | solution.py:29
  101.8 1.2 fusion.187
  103.7 1.2 fusion.187
  105.6 1.2 fusion.187
  106.8 64.7 %all-gather.10.cloned.1.call-done = bf16[3,768,768]{2,1,0:T(8,128)(2,1)} async-done(((bf16[3,192,768]{2,1,0:T(8,128)(2,1)}), bf16[3,768,768]{2,1,0:T(8,128)(2,1)}) %all-gather.10.cloned.1.call-update) | async-done | bytes 3538960 | tf_op jit(solution)/shard_map/all_gather | solution.py:155
  171.5 3.3 fusion.71
  174.8 1.5 copy.104
  176.3 3.5 fusion.74
  180.2 27.0 %while.66 = (s32[]{:T(128)}, f32[3,1,6,64,128]{4,3,2,0,1:T(8,128)S(1)}, bf16[3,1,256,6,128]{2,4,3,0,1:T(8,128)(2,1)S(1)}, f32[2,3,1,6,64,128]{5,4,3,1,2,0:T(8,12...) while((s32[]{:T(128)}, ...), condition=%wide.region_8.9_spmd, body=%wide.region_6.8_spmd.sunk | while | flops 946094080 | bytes 10168943 | solution.py:102
  180.2 1.3 constant_dynamic-slice_fusion.10
  181.5 1.9 reduce_window_sum.68
  183.7 0.9 dynamic-slice_bitcast_fusion.6
  184.6 2.0 convolution_bitcast_fusion.8
  187.1 3.9 fusion.159
  191.2 2.5 fusion.157
  193.7 1.3 constant_dynamic-slice_fusion.10
  195.0 1.9 reduce_window_sum.68
  197.2 0.9 dynamic-slice_bitcast_fusion.6
  198.1 2.0 convolution_bitcast_fusion.8
  200.6 3.9 fusion.159
  204.6 2.5 fusion.157
  207.2 5.7 %fusion.82 = f32[3,768,768]{2,1,0:T(8,128)} fusion(bf16[3,256,768]{1,2,0:T(8,128)(2,1)S(1)} %bitcast.282, bf16[1,1,256,768]{3,2,0,1:T(8,128)(2,1)} %bitcast.290, bf16[1,1,256,768]{3,2,0,1:T(8,128)(2,1)S(1)} %bitcast.288, bf16[1,1,256,768]{3,2,0,1:T(8,128)(2,1)} %bitcast.292), kind=kOutput, calls=%fused_computation.120 | convolution fusion | flops 907149312 | bytes 9437184 | tf_op jit(solution)/shard_map/ovtd,ovti->odi/dot_general | solution.py:187
  214.2 1.8 copy.109
  216.0 13.1 %all-gather.12.cloned.1.call-done = f32[12,6,64,128]{3,2,1,0:T(8,128)} async-done(((f32[3,6,64,128]{3,2,1,0:T(8,128)}), f32[12,6,64,128]{3,2,1,0:T(8,128)}) %all-gather.12.cloned.1.call-update) | async-done | bytes 2359312 | tf_op jit(solution)/shard_map/all_gather | solution.py:17
  229.1 1.8 rev.6
  231.7 0.7 broadcast.217
  233.1 41.1 %while.67 = (s32[]{:T(128)}, f32[3,1,6,64,128]{4,3,2,0,1:T(8,128)S(1)}, bf16[3,1,256,6,128]{2,4,3,0,1:T(8,128)(2,1)S(1)}, f32[3,1,256,64]{2,3,0,1:T(8,128)}, f32...) while((s32[]{:T(128)}, ...), condition=%wide.region_12.13_spmd, body=%wide.region_9.12_spmd.sunk | while | flops 1929625600 | bytes 41488220 | solution.py:123
  233.1 0.9 reduce_window_sum.69
  234.1 1.1 dynamic-slice_bitcast_fusion.7
  235.2 2.0 convolution_bitcast_fusion.9
  237.9 1.7 fusion.178
  239.6 1.0 copy-done.5
  241.0 2.3 fusion.182
  243.3 3.7 fusion.180
  247.5 2.6 fusion.179
  250.2 2.4 fusion.176
  252.6 0.9 fusion.181
  253.6 0.8 reduce_window_sum.69
  254.6 1.1 dynamic-slice_bitcast_fusion.7
  255.7 2.0 convolution_bitcast_fusion.9
  258.4 1.7 fusion.178
  260.1 1.0 copy-done.5
  261.5 2.3 fusion.182
  263.8 3.7 fusion.180
  268.0 2.7 fusion.179
  270.7 2.4 fusion.176
  273.2 0.9 fusion.181
  274.1 1.1 copy.121
  275.2 1.1 copy.122
  276.5 1.5 copy.125
  278.0 5.0 %all-reduce.2 = bf16[3,1,256,128]{3,2,1,0:T(8,128)(2,1)} all-reduce(f32[3,1,256,128]{3,2,1,0:T(8,128)S(1)} %pad_maximum_fusion), channel_id=1, replica_groups=mesh['groups'=2,'ctx'=4,'dp'=2,'mp'=2] {'mp'}, use_global_device_ids=true, to_apply=%region_13.14 | all-reduce | flops 98304 | bytes 589824 | tf_op jit(solution)/shard_map/psum | solution.py:182
  283.0 70.6 %reduce-scatter.2.cloned.1.call-done = f32[3,192,768]{2,1,0:T(8,128)} async-done(((f32[3,768,768]{2,1,0:T(8,128)}), f32[3,192,768]{2,1,0:T(8,128)}) %reduce-scatter.2.cloned.1.call-update) | async-done | bytes 1769488 | tf_op jit(solution)/shard_map/reduce_scatter | solution.py:190
  353.6 46.3 %all-reduce.3 = bf16[3,192,768]{2,1,0:T(8,128)(2,1)} all-reduce(f32[3,192,768]{2,1,0:T(8,128)} %reduce-scatter.2.cloned.1.call-done), channel_id=1, replica_groups=mesh['groups'=2,'ctx'=4,'dp'=2,'mp'=2] {'dp'}, use_global_device_ids=true, to_apply=%region_15.16 | all-reduce | flops 442368 | bytes 2654208 | tf_op jit(solution)/shard_map/psum | solution.py:191
  (121 shorter events, 14.7 us)
Async XLA Ops:
  7.2 8.9 %copy-start.10 = (bf16[3,1,256,768]{3,2,1,0:T(8,128)(2,1)S(1)}, bf16[3,1,256,768]{3,2,1,0:T(8,128)(2,1)}, u32[]{:S(2)}) copy-start(bf16[3,1,256,768]{3,2,1,0:T(8,128)(2,1)} %param.14) | copy-start | bytes 3538948
  7.2 42.4 %all-gather.8.cloned.1.call-start = ((), (), s32[]{:S(2)}) async-start(), calls=%async_computation.1 | async-start | bytes 1966080 | tf_op jit(solution)/shard_map/all_gather | solution.py:146
  7.9 93.2 %all-gather.14.cloned.1.call-start = ((), (), s32[]{:S(2)}) async-start(), calls=%async_computation.5 | async-start | bytes 2949120 | tf_op jit(solution)/shard_map/all_gather | solution.py:17
  8.7 8.0 %copy-start.8 = (f32[3,1,6,256]{3,2,1,0:T(8,128)}, f32[3,1,6,256]{3,2,1,0:T(8,128)S(1)}, u32[]{:S(2)}) copy-start(f32[3,1,6,256]{3,2,1,0:T(8,128)S(1)} %fusion.84) | copy-start | bytes 55300
  20.6 150.9 %all-gather.10.cloned.1.call-start = ((), (), s32[]{:S(2)}) async-start(), calls=%async_computation.2 | async-start | bytes 4423680 | tf_op jit(solution)/shard_map/all_gather | solution.py:155
  21.3 207.8 %all-gather.12.cloned.1.call-start = ((), (), s32[]{:S(2)}) async-start(), calls=%async_computation.4 | async-start | bytes 2949120 | tf_op jit(solution)/shard_map/all_gather | solution.py:17
  21.5 15.8 %copy-start.14 = (s32[2,1,256]{2,1,0:T(1,128)S(1)}, s32[2,1,256]{2,1,0:T(1,128)}, u32[]{:S(2)}) copy-start(s32[2,1,256]{2,1,0:T(1,128)} %param.17) | copy-start | bytes 6148
  49.6 3.7 copy-start.1
  101.1 70.4 %copy-start.7 = (bf16[256,768]{1,0:T(8,128)(2,1)S(1)}, bf16[256,768]{1,0:T(8,128)(2,1)}, u32[]{:S(2)}) copy-start(bf16[256,768]{1,0:T(8,128)(2,1)} %gather_fusion) | copy-start | bytes 1179652
  174.8 1.5 copy-start.3
  179.8 173.8 %reduce-scatter.2.cloned.1.call-start = ((), (), s32[]{:S(2)}) async-start(), calls=%async_computation.3 | async-start | bytes 8847360 | tf_op jit(solution)/shard_map/reduce_scatter | solution.py:190
  207.2 5.8 %copy-start.2 = (f32[2,3,1,6,64,128]{5,4,3,1,2,0:T(8,128)}, f32[2,3,1,6,64,128]{5,4,3,1,2,0:T(8,128)S(1)}, u32[]{:S(2)}) copy-start(f32[2,3,1,6,64,128]{5,4,3,1,2,0:T(8,128)S(1)} %get-tuple-element.1132) | copy-start | bytes 3538948
  212.9 0.7 copy-start.13
  212.9 1.3 copy-start.4
  231.5 1.5 copy-start.9
  234.1 3.6 copy-start
  239.6 1.0 copy-start.5
  243.3 3.7 copy-start.11
  247.5 2.6 copy-start.12
  250.2 3.4 copy-start.6
  254.6 3.6 copy-start
  260.1 1.0 copy-start.5
  263.8 3.7 copy-start.11
  268.0 2.7 copy-start.12
  270.7 3.4 copy-start.6
Sparse Core Ops, SparseCore 0:
  9.6 39.9 all-gather.7
  51.7 49.3 all-gather.13
  102.7 68.7 all-gather.9
  180.0 49.1 all-gather.11
  231.3 122.3 reduce-scatter.1
where the time goes:
time: 408 us; the launch traced here: 406 us
  waiting for transfers between devices  207 us (51%)
  matrix products  66.1 us (16%)
  blocking collectives  65.4 us (16%)
  local copies, waits for them, and re-layouts  35.1 us (9%)
  other arithmetic  18 us (4%)
  between operations  14 us (3%)
    reduce_scatter x1, waiting for transfers between devices, shards(): lax.psum_scatter(weight_term, 'ctx', scatter_dimension=1, tiled=True)  70.6 us
    all_gather x1, waiting for transfers between devices, shards(): lax.all_gather(out_weight, 'ctx', axis=1, tiled=True)  64.7 us
    all_gather x2, waiting for transfers between devices, prefix(): pieces = jax.tree.map(lambda part: lax.all_gather(part, axis), value)  58.1 us
    dot_general x28, matrix products, contract(): return jnp.einsum(form, *operands, precision=EXACT)  57 us
    psum x1, blocking collectives, shards(): weight_grad = lax.psum(rows_sum, 'dp').astype(jnp.bfloat16)  46.3 us
    all_gather x1, blocking collectives, prefix(): pieces = jax.tree.map(lambda part: lax.all_gather(part, axis), value)  14.1 us
    all_gather x1, waiting for transfers between devices, shards(): gathered = lax.all_gather(cotangent, 'ctx', axis=1, tiled=True)  12.2 us
  transfers between devices with their start and end apart: 5, of which 5 were waited for; matrix products, arithmetic and copies ran while one was open for 26% of the time, Pallas kernels for 0%

commit v1 on v0

v1 whole, which is shorter than its diff:
```python
import functools
import math

import jax
import jax.numpy as jnp
from jax import lax
from jax.experimental import pallas as pl
from jax.experimental.pallas import tpu as pltpu
from jax.sharding import PartitionSpec as P

P_SIZE = 128
N = 64
F32 = jnp.float32
BF = jnp.bfloat16
MESH = pl.DeviceIdType.MESH


def dot(a, b, ca, cb):
    return lax.dot_general(a, b, (((ca,), (cb,)), ((), ())), preferred_element_type=F32)


def kernel(
    sizes, x_ref, wr_ref, steps_ref, orders_ref, cot_ref, w_ref,
    gx_ref, gwr_ref, gw_ref,
    sums, sums_in, cotg, wg, ends, ends_in, state, grads, grads_in, gout, scanned, mixing, outs, dys,
    pf, pb, pa_in, sb, sb_in, cb, cb_in, runc, runr, part, part_in,
    s_sum, r_sum, s_cot, r_cot, s_w, r_w, s_g, r_g, s_end, r_end, s_gr, r_gr, s_a, r_a, s_b, r_b,
    s_c, r_c, s_m, r_m,
):
    n, n_dp, n_gr, n_mp = sizes
    me = lax.axis_index("ctx")
    my_dp = lax.axis_index("dp")
    my_gr = lax.axis_index("groups")
    my_mp = lax.axis_index("mp")
    tokens, width = cot_ref.shape
    inner = x_ref.shape[2]
    heads = inner // P_SIZE
    rows = w_ref.shape[1]
    blk = tokens // n
    seq = tokens * n
    scale = -1.0 / seq
    wcol = inner // n_gr
    parts = math.gcd(inner // 128, n_dp)
    pcol = inner // parts

    def ctx_at(k):
        return lax.rem(me + k, n)

    def gr_at(k):
        return lax.rem(my_gr + k, n_gr)

    def dp_at(k):
        return lax.rem(my_dp + k, n_dp)

    my_part = lax.rem(my_dp, parts)
    base_dp = my_dp - my_part

    def pair_at(k):
        return base_dp + lax.rem(my_part + k, parts)

    def send(src, dst, ss, rs, where):
        return pltpu.make_async_remote_copy(
            src_ref=src, dst_ref=dst, send_sem=ss, recv_sem=rs, device_id=where, device_id_type=MESH
        )

    barrier = pltpu.get_barrier_semaphore()
    for k in range(1, n):
        pl.semaphore_signal(barrier, inc=1, device_id={"ctx": ctx_at(k)}, device_id_type=MESH)
    for k in range(1, n_gr):
        pl.semaphore_signal(barrier, inc=1, device_id={"groups": gr_at(k)}, device_id_type=MESH)
    for k in range(1, n_dp):
        pl.semaphore_signal(barrier, inc=1, device_id={"dp": dp_at(k)}, device_id_type=MESH)
    for k in range(1, n_mp):
        pl.semaphore_signal(barrier, inc=1, device_id={"mp": lax.rem(my_mp + k, n_mp)}, device_id_type=MESH)
    pl.semaphore_wait(barrier, n + n_gr + n_dp + n_mp - 4)

    def cot_copy(k):
        return send(
            cot_ref.at[pl.ds(pl.multiple_of(ctx_at(k) * blk, blk), blk)],
            cotg.at[pl.ds(pl.multiple_of(me * blk, blk), blk)],
            s_cot.at[k], r_cot.at[k], {"ctx": ctx_at(k)},
        )

    def w_copy(k):
        cols = pl.ds(pl.multiple_of(my_gr * wcol, 128), wcol)
        return send(
            w_ref.at[:, :, cols],
            wg.at[:, pl.ds(pl.multiple_of(me * rows, rows), rows), cols],
            s_w.at[k], r_w.at[k], {"ctx": ctx_at(k)},
        )

    def g_copy(k, g):
        owner = lax.rem(me + n - k, n)
        piece = wg.at[
            :, pl.ds(pl.multiple_of(owner * rows, rows), rows), pl.ds(pl.multiple_of(my_gr * wcol, 128), wcol)
        ]
        return send(piece, piece, s_g.at[k, g], r_g.at[k, g], {"groups": gr_at(g)})

    def sum_copy(k):
        return send(sums, sums_in.at[k], s_sum.at[k], r_sum.at[k], {"ctx": ctx_at(k)})

    for k in range(1, n):
        cot_copy(k).start()
    lower = (
        lax.broadcasted_iota(jnp.int32, (tokens, tokens), 0)
        >= lax.broadcasted_iota(jnp.int32, (tokens, tokens), 1)
    )
    tri = jnp.where(lower, 1.0, 0.0).astype(BF)

    def running(o, _):
        steps = steps_ref[o]
        high = (steps // 256).astype(F32).astype(BF)
        low = (steps % 256).astype(F32).astype(BF)
        runr[o] = dot(high, tri, 1, 1) * 256.0 + dot(low, tri, 1, 1)
        runc[o] = dot(tri, high, 1, 1) * 256.0 + dot(tri, low, 1, 1)
        sums[o] = jnp.broadcast_to(runr[o][:, tokens - 1 :] * scale, sums.shape[1:])
        return 0

    lax.fori_loop(0, 3, running, 0)
    for k in range(1, n):
        sum_copy(k).start()
    for k in range(1, n):
        w_copy(k).start()

    def end_states(o, _):
        bt = wr_ref[o][:, :N]
        rc = runc[o] * scale
        falling = jnp.exp(rc[tokens - 1 :, :] - rc)
        for h in range(heads):
            xs = (x_ref[o, :, h * P_SIZE : (h + 1) * P_SIZE].astype(F32) * falling[:, h : h + 1]).astype(BF)
            ends[o, h] = dot(bt, xs, 0, 0).astype(BF)
        return 0

    lax.fori_loop(0, 3, end_states, 0)

    def end_copy(k):
        return send(ends, ends_in.at[k], s_end.at[k], r_end.at[k], {"ctx": ctx_at(k)})

    def grad_copy(k):
        return send(grads, grads_in.at[k], s_gr.at[k], r_gr.at[k], {"ctx": lax.rem(me + n - k, n)})

    for k in range(1, n):

        @pl.when(me + k < n)
        def _():
            end_copy(k).start()

    cotg[pl.ds(pl.multiple_of(me * blk, blk), blk), :] = cot_ref[pl.ds(pl.multiple_of(me * blk, blk), blk), :]
    wg[:, pl.ds(pl.multiple_of(me * rows, rows), rows), :] = w_ref[...]
    for k in range(1, n):
        cot_copy(k).wait()
    scanned[0] = cot_ref[...]

    def permute(o, _):
        ids = orders_ref[o]
        place = (ids // tokens) * blk + ids % blk
        hot = jnp.where(lax.broadcasted_iota(jnp.int32, (tokens, tokens), 0) == place, 1.0, 0.0).astype(BF)
        scanned[o + 1] = dot(hot, cotg[...], 0, 0).astype(BF)
        return 0

    lax.fori_loop(0, 2, permute, 0)

    state[...] = jnp.zeros_like(state)
    gout[...] = jnp.zeros_like(gout)
    for k in range(1, n):
        sum_copy(k).wait()

    def gather_states(total, got, copy_of, mine, sums_at):
        for k in range(1, n):

            @pl.when(mine >= k)
            def _():
                copy_of(k).wait_recv()

                def one(o, _):
                    log = jnp.zeros(sums.shape[1:], F32)
                    for j in range(1, k):
                        log = log + sums_in[sums_at(j), o]
                    fade = jnp.exp(log)
                    for h in range(heads):
                        total[o, h] = total[o, h] + fade[h : h + 1, :] * got[k, o, h].astype(F32)
                    return 0

                lax.fori_loop(0, 3, one, 0)

    gather_states(state, ends_in, end_copy, me, lambda j: j)

    def pair_copy(k, o):
        cols = pl.ds(pl.multiple_of((pair_at(k) - base_dp) * pcol, 128), pcol)
        return send(
            pb.at[o, :, cols], pa_in.at[k, o], s_a.at[k, o], r_a.at[k, o], {"dp": pair_at(k)}
        )

    def forward(o, _):
        bt = wr_ref[o][:, :N]
        ct = wr_ref[o][:, N:]
        scores = dot(ct, bt, 1, 1)
        rc = runc[o] * scale
        rr = runr[o] * scale
        rising = jnp.exp(rc)
        for h in range(heads):
            cut = slice(h * P_SIZE, (h + 1) * P_SIZE)
            decay = jnp.where(lower, jnp.exp(jnp.minimum(rc[:, h : h + 1] - rr[h : h + 1, :], 0.0)), 0.0)
            mix = (scores * decay).astype(BF)
            mixing[o, h] = mix
            up = (ct.astype(F32) * rising[:, h : h + 1]).astype(BF)
            outs[:, cut] = (
                dot(mix, x_ref[o, :, cut], 1, 0) + dot(up, state[o, h].astype(BF), 1, 0)
            ).astype(BF)
        term = dot(scanned[o], outs[...], 0, 0)
        pf[o] = term
        pb[o] = term.astype(BF)
        for k in range(1, parts):
            pair_copy(k, o).start()
        return 0

    lax.fori_loop(0, 3, forward, 0)

    for k in range(1, n):
        w_copy(k).wait()
        for g in range(1, n_gr):
            g_copy(k, g).start()
    for k in range(1, n):
        for g in range(1, n_gr):
            g_copy(k, g).wait()

    def upstream(o, _):
        ct = wr_ref[o][:, N:]
        dys[o] = dot(scanned[o], wg[o], 1, 0).astype(BF)
        rising = jnp.exp(runc[o] * scale)
        for h in range(heads):
            up = (ct.astype(F32) * rising[:, h : h + 1]).astype(BF)
            grads[o, h] = dot(up, dys[o, :, h * P_SIZE : (h + 1) * P_SIZE], 0, 0).astype(BF)
        return 0

    lax.fori_loop(0, 3, upstream, 0)
    for k in range(1, n):

        @pl.when(me >= k)
        def _():
            grad_copy(k).start()

    mine_cols = pl.ds(pl.multiple_of(my_part * pcol, 128), pcol)

    def ctx_copy(k, o):
        return send(
            sb.at[o, pl.ds(pl.multiple_of(ctx_at(k) * rows, rows), rows)],
            sb_in.at[k, o], s_b.at[k, o], r_b.at[k, o], {"ctx": ctx_at(k)},
        )

    def pair_sum(o, _):
        total = pf[o, :, mine_cols]
        for k in range(1, parts):
            pair_copy(k, o).wait()
            total = total + pa_in[k, o].astype(F32)
        pf[o, :, mine_cols] = total
        sb[o] = total.astype(BF)
        for k in range(1, n):
            ctx_copy(k, o).start()
        return 0

    lax.fori_loop(0, 3, pair_sum, 0)
    gather_states(gout, grads_in, grad_copy, n - 1 - me, lambda j: n - j)

    def backward(o, _):
        bt = wr_ref[o][:, :N]
        ct = wr_ref[o][:, N:]
        rc = runc[o] * scale
        rr = runr[o] * scale
        rising = jnp.exp(rc)
        falling = jnp.exp(rc[tokens - 1 :, :] - rc)
        both = jnp.zeros((tokens, tokens), F32)
        gb = jnp.zeros((tokens, N), F32)
        gc = jnp.zeros((tokens, N), F32)
        for h in range(heads):
            cut = slice(h * P_SIZE, (h + 1) * P_SIZE)
            xs = x_ref[o, :, cut]
            dy = dys[o, :, cut]
            far = gout[o, h].astype(BF)
            down = (bt.astype(F32) * falling[:, h : h + 1]).astype(BF)
            gx_ref[o, :, cut] = (dot(mixing[o, h], dy, 0, 0) + dot(down, far, 1, 0)).astype(BF)
            decay = jnp.where(lower, jnp.exp(jnp.minimum(rc[:, h : h + 1] - rr[h : h + 1, :], 0.0)), 0.0)
            both = both + dot(dy, xs, 1, 1) * decay
            gb = gb + falling[:, h : h + 1] * dot(xs, far, 1, 1)
            gc = gc + rising[:, h : h + 1] * dot(dy, state[o, h].astype(BF), 1, 1)
        both = both.astype(BF)
        part[o, :, :N] = gb + dot(both, ct, 0, 0)
        part[o, :, N:] = gc + dot(both, bt, 1, 0)
        return 0

    lax.fori_loop(0, 3, backward, 0)

    def mp_copy(k):
        return send(part, part_in.at[k], s_m.at[k], r_m.at[k], {"mp": lax.rem(my_mp + k, n_mp)})

    for k in range(1, n_mp):
        mp_copy(k).start()

    def dp_copy(k):
        return send(cb, cb_in.at[k], s_c.at[k], r_c.at[k], {"dp": dp_at(k)})

    def ctx_sum(o, _):
        total = pf[o, pl.ds(pl.multiple_of(me * rows, rows), rows), mine_cols]
        for k in range(1, n):
            ctx_copy(k, o).wait()
            total = total + sb_in[k, o].astype(F32)
        cb[o] = total.astype(BF)
        return 0

    lax.fori_loop(0, 3, ctx_sum, 0)
    for k in range(1, n_dp):
        dp_copy(k).start()
    for k in range(1, n_mp):
        mp_copy(k).wait()
    total = part[...]
    for k in range(1, n_mp):
        total = total + part_in[k]
    gwr_ref[...] = total.astype(BF)
    for k in range(1, n_dp):
        dp_copy(k).wait()
    for u in range(parts):
        sum_u = jnp.zeros((3, rows, pcol), F32)
        own = cb[...].astype(F32)
        for k in range(n_dp):
            piece = own if k == 0 else cb_in[k].astype(F32)
            belongs = lax.rem(my_dp + n_dp - k, parts) == u
            sum_u = sum_u + jnp.where(belongs, piece, 0.0)
        gw_ref[:, :, u * pcol : (u + 1) * pcol] = sum_u.astype(BF)

    for k in range(1, n):

        @pl.when(me + k < n)
        def _():
            end_copy(k).wait_send()

        @pl.when(me >= k)
        def _():
            grad_copy(k).wait_send()


def shards(sizes, head_inputs, write_read, decay_steps, scan_orders, cotangent, out_weight):
    n, n_dp, n_gr, n_mp = sizes
    tokens, width = cotangent.shape[1:]
    inner = head_inputs.shape[3]
    heads = decay_steps.shape[2]
    rows = out_weight.shape[1]
    parts = math.gcd(inner // 128, n_dp)
    pcol = inner // parts
    x = head_inputs.reshape(3, tokens, inner)
    wr = write_read.reshape(3, tokens, 2 * N)
    steps = jnp.pad(decay_steps.reshape(3, heads, tokens), ((0, 0), (0, -heads % 8), (0, 0)))
    hp = steps.shape[1]
    V = pltpu.VMEM
    dma = pltpu.SemaphoreType.DMA
    scratch = [
        V((3, hp, 128), F32), V((n, 3, hp, 128), F32), V((tokens, width), BF), V((3, width, inner), BF),
        V((3, heads, N, P_SIZE), BF), V((n, 3, heads, N, P_SIZE), BF), V((3, heads, N, P_SIZE), F32),
        V((3, heads, N, P_SIZE), BF), V((n, 3, heads, N, P_SIZE), BF), V((3, heads, N, P_SIZE), F32),
        V((3, tokens, width), BF), V((3, heads, tokens, tokens), BF), V((tokens, inner), BF),
        V((3, tokens, inner), BF),
        V((3, width, inner), F32), V((3, width, inner), BF), V((parts, 3, width, pcol), BF),
        V((3, width, pcol), BF), V((n, 3, rows, pcol), BF), V((3, rows, pcol), BF), V((n_dp, 3, rows, pcol), BF),
        V((3, tokens, hp), F32), V((3, hp, tokens), F32),
        V((3, tokens, 2 * N), F32), V((n_mp, 3, tokens, 2 * N), F32),
        dma((n,)), dma((n,)), dma((n,)), dma((n,)), dma((n,)), dma((n,)), dma((n, n_gr)), dma((n, n_gr)),
        dma((n,)), dma((n,)), dma((n,)), dma((n,)), dma((parts, 3)), dma((parts, 3)), dma((n, 3)), dma((n, 3)),
        dma((n_dp,)), dma((n_dp,)), dma((n_mp,)), dma((n_mp,)),
    ]
    gx, gwr, gw = pl.pallas_call(
        functools.partial(kernel, sizes),
        out_shape=(
            jax.ShapeDtypeStruct((3, tokens, inner), BF),
            jax.ShapeDtypeStruct((3, tokens, 2 * N), BF),
            jax.ShapeDtypeStruct((3, rows, inner), BF),
        ),
        in_specs=[pl.BlockSpec(memory_space=V)] * 6,
        out_specs=(pl.BlockSpec(memory_space=V),) * 3,
        scratch_shapes=scratch,
        compiler_params=pltpu.CompilerParams(
            collective_id=0, has_side_effects=True, vmem_limit_bytes=60 * 2**20
        ),
    )(x, wr, steps, scan_orders.reshape(2, 1, tokens), cotangent.reshape(tokens, width), out_weight)
    return gx[:, None], gwr[:, None], gw


def solution(mesh):
    sizes = (mesh.shape["ctx"], mesh.shape["dp"], mesh.shape["groups"], mesh.shape["mp"])
    in_specs = (
        P(None, ("groups", "dp"), "ctx", "mp"),
        P(None, ("groups", "dp"), "ctx", None),
        P(None, ("groups", "dp"), "mp", "ctx"),
        P(None, ("groups", "dp"), "ctx"),
        P(("groups", "dp"), "ctx", None),
        P(None, "ctx", "mp"),
    )
    out_specs = (
        P(None, ("groups", "dp"), "ctx", "mp"),
        P(None, ("groups", "dp"), "ctx", None),
        P("groups", "ctx", "mp"),
    )
    return jax.shard_map(
        functools.partial(shards, sizes), mesh=mesh, in_specs=in_specs, out_specs=out_specs, check_vma=False
    )
```

time: 408 us -> 188 us (0.46)
  waiting for transfers between devices: 207 us -> 0 us
  Pallas kernels: 0 us -> 181 us
  matrix products: 66.1 us -> 0 us
  blocking collectives: 65.4 us -> 0 us
  local copies, waits for them, and re-layouts: 35.1 us -> 5.39 us
  other arithmetic: 18 us -> 0 us
  between operations: 14 us -> 0.66 us
    pallas_call x0 -> x1, Pallas kernels: none -> 181 us  [shards(): pl.pallas_call(functools.partial(kernel, sizes), out_shape=(jax.ShapeDtyp...]
    all_gather x4 -> x0, waiting for transfers between devices: 135 us -> none  [the longest x1 64.7 us: shards(): lax.all_gather(out_weight, 'ctx', axis=1, tiled=True)]
    reduce_scatter x1 -> x0, waiting for transfers between devices: 70.6 us -> none  [shards(): lax.psum_scatter(weight_term, 'ctx', scatter_dimension=1, tiled=True)]
    dot_general x30 -> x0, matrix products: 66.1 us -> none  [the longest x28 57 us: contract(): return jnp.einsum(form, *operands, precision=EXACT)]
    psum x2 -> x0, blocking collectives: 51.3 us -> none  [the longest x1 46.3 us: shards(): weight_grad = lax.psum(rows_sum, 'dp').astype(jnp.bfloat16)]
    all_gather x1 -> x0, blocking collectives: 14.1 us -> none  [prefix(): pieces = jax.tree.map(lambda part: lax.all_gather(part, axis), value)]
    another operation x7 -> x0, other arithmetic: 11.8 us -> none
    gather x3 -> x0, local copies, waits for them, and re-layouts: 6.56 us -> none  [reorder(): table_rows[row_ids]]
  transfers between devices with their start and end apart: 5 -> 0, of which waited for: 5 -> 0; matrix products, arithmetic and copies ran while one was open for 26% -> 0% of each run, Pallas kernels for 0% -> 0%
where the time goes in v1:
time: 188 us
  Pallas kernels  181 us (96%)
  local copies, waits for them, and re-layouts  5.39 us (3%)
    pallas_call x1, Pallas kernels, shards(): pl.pallas_call(functools.partial(kernel, sizes), out_shape=(jax.ShapeDtyp...  181 us
    unnamed x8, local copies, waits for them, and re-layouts  4.78 us

profile of v1, /device:TPU:0, one launch (start us, length us, event | category | flops | bytes accessed | tf_op | source)
XLA Modules:
  0.0 187.5 jit_solution(5236090961653763902)
XLA Ops:
  0.6 0.7 copy.13
  1.4 0.6 pad.4.steps_ref
  2.0 181.5 %shard_map.85 = (bf16[3,256,768]{2,1,0:T(8,128)(2,1)}, bf16[3,256,128]{2,1,0:T(8,128)(2,1)}, bf16[3,192,768]{2,1,0:T(8,128)(2,1)}) custom-call(bf16[3,256,768]{2,1,0:T(8,128)(2,1)} %bitcast.12, bf16[3,256,128]{2,1,0:T(8,128)(2,1)} %bitcast.15, s32[3,8,256]{2,1,0:T(8,128)} %pad.4.steps_ref, s32[2,1,256]{2,1,0:T(1,128)} %orders_ref.1, ...), custom_call_target="tpu_custom_call" | custom-call | tf_op jit(solution)/shard_map/pallas_call | solution.py:369
  183.4 0.0 copy-start.1
  183.5 0.0 copy-start
  183.5 2.4 %copy.17 = bf16[3,1,256,768]{3,2,1,0:T(8,128)(2,1)} copy(bf16[3,1,256,768]{3,2,1,0:T(8,128)(2,1)} %bitcast.13) | data formatting | bytes 2359296
  185.9 0.0 copy-done.1
  185.9 0.7 copy.18
  186.6 0.0 copy-done
  186.6 0.9 copy.19
Async XLA Ops:
  183.4 2.5 %copy-start.1 = (bf16[3,256,128]{2,1,0:T(8,128)(2,1)S(1)}, bf16[3,256,128]{2,1,0:T(8,128)(2,1)}, u32[]{:S(2)}) copy-start(bf16[3,256,128]{2,1,0:T(8,128)(2,1)} %get-tuple-element.7) | copy-start | bytes 589828
  183.5 3.1 %copy-start = (bf16[3,192,768]{2,1,0:T(8,128)(2,1)S(1)}, bf16[3,192,768]{2,1,0:T(8,128)(2,1)}, u32[]{:S(2)}) copy-start(bf16[3,192,768]{2,1,0:T(8,128)(2,1)} %get-tuple-element.17) | copy-start | bytes 2654212

commit v2 on v1

--- a/solution.py
+++ b/solution.py
@@ -22,9 +22,9 @@
 def kernel(
     sizes, x_ref, wr_ref, steps_ref, orders_ref, cot_ref, w_ref,
     gx_ref, gwr_ref, gw_ref,
-    sums, sums_in, cotg, wg, ends, ends_in, state, grads, grads_in, gout, scanned, mixing, outs, dys,
+    cotg, wg, ends, ends_out, ends_in, state, grads, grads_out, grads_in, gout, scanned, mixing, outs, dys,
     pf, pb, pa_in, sb, sb_in, cb, cb_in, runc, runr, part, part_in,
-    s_sum, r_sum, s_cot, r_cot, s_w, r_w, s_g, r_g, s_end, r_end, s_gr, r_gr, s_a, r_a, s_b, r_b,
+    s_cot, r_cot, s_w, r_w, s_g, r_g, s_end, r_end, s_gr, r_gr, s_a, r_a, s_b, r_b,
     s_c, r_c, s_m, r_m,
 ):
     n, n_dp, n_gr, n_mp = sizes
@@ -96,11 +96,10 @@
         ]
         return send(piece, piece, s_g.at[k, g], r_g.at[k, g], {"groups": gr_at(g)})
 
-    def sum_copy(k):
-        return send(sums, sums_in.at[k], s_sum.at[k], r_sum.at[k], {"ctx": ctx_at(k)})
-
     for k in range(1, n):
         cot_copy(k).start()
+    for k in range(1, n):
+        w_copy(k).start()
     lower = (
         lax.broadcasted_iota(jnp.int32, (tokens, tokens), 0)
         >= lax.broadcasted_iota(jnp.int32, (tokens, tokens), 1)
@@ -113,14 +112,9 @@
         low = (steps % 256).astype(F32).astype(BF)
         runr[o] = dot(high, tri, 1, 1) * 256.0 + dot(low, tri, 1, 1)
         runc[o] = dot(tri, high, 1, 1) * 256.0 + dot(tri, low, 1, 1)
-        sums[o] = jnp.broadcast_to(runr[o][:, tokens - 1 :] * scale, sums.shape[1:])
         return 0
 
     lax.fori_loop(0, 3, running, 0)
-    for k in range(1, n):
-        sum_copy(k).start()
-    for k in range(1, n):
-        w_copy(k).start()
 
     def end_states(o, _):
         bt = wr_ref[o][:, :N]
@@ -128,22 +122,29 @@
         falling = jnp.exp(rc[tokens - 1 :, :] - rc)
         for h in range(heads):
             xs = (x_ref[o, :, h * P_SIZE : (h + 1) * P_SIZE].astype(F32) * falling[:, h : h + 1]).astype(BF)
-            ends[o, h] = dot(bt, xs, 0, 0).astype(BF)
+            ends[o, h] = dot(bt, xs, 0, 0)
         return 0
 
     lax.fori_loop(0, 3, end_states, 0)
 
-    def end_copy(k):
-        return send(ends, ends_in.at[k], s_end.at[k], r_end.at[k], {"ctx": ctx_at(k)})
-
-    def grad_copy(k):
-        return send(grads, grads_in.at[k], s_gr.at[k], r_gr.at[k], {"ctx": lax.rem(me + n - k, n)})
-
-    for k in range(1, n):
-
-        @pl.when(me + k < n)
-        def _():
-            end_copy(k).start()
+    def end_copy(o):
+        return send(ends_out.at[o], ends_in.at[o], s_end.at[o], r_end.at[o], {"ctx": lax.rem(me + 1, n)})
+
+    def grad_copy(o):
+        return send(grads_out.at[o], grads_in.at[o], s_gr.at[o], r_gr.at[o], {"ctx": lax.rem(me + n - 1, n)})
+
+    def chain(o, copy_of, total, own, outgoing, incoming, first, last):
+        @pl.when(jnp.logical_not(first))
+        def _():
+            copy_of(o).wait_recv()
+            total[o] = incoming[o].astype(F32)
+
+        @pl.when(jnp.logical_not(last))
+        def _():
+            fade = jnp.exp(runr[o][:, tokens - 1 :] * scale)
+            for h in range(heads):
+                outgoing[o, h] = (total[o, h] * fade[h : h + 1, :] + own[o, h]).astype(outgoing.dtype)
+            copy_of(o).start()
 
     cotg[pl.ds(pl.multiple_of(me * blk, blk), blk), :] = cot_ref[pl.ds(pl.multiple_of(me * blk, blk), blk), :]
     wg[:, pl.ds(pl.multiple_of(me * rows, rows), rows), :] = w_ref[...]
@@ -162,29 +163,6 @@
 
     state[...] = jnp.zeros_like(state)
     gout[...] = jnp.zeros_like(gout)
-    for k in range(1, n):
-        sum_copy(k).wait()
-
-    def gather_states(total, got, copy_of, mine, sums_at):
-        for k in range(1, n):
-
-            @pl.when(mine >= k)
-            def _():
-                copy_of(k).wait_recv()
-
-                def one(o, _):
-                    log = jnp.zeros(sums.shape[1:], F32)
-                    for j in range(1, k):
-                        log = log + sums_in[sums_at(j), o]
-                    fade = jnp.exp(log)
-                    for h in range(heads):
-                        total[o, h] = total[o, h] + fade[h : h + 1, :] * got[k, o, h].astype(F32)
-                    return 0
-
-                lax.fori_loop(0, 3, one, 0)
-
-    gather_states(state, ends_in, end_copy, me, lambda j: j)
-
     def pair_copy(k, o):
         cols = pl.ds(pl.multiple_of((pair_at(k) - base_dp) * pcol, 128), pcol)
         return send(
@@ -192,6 +170,7 @@
         )
 
     def forward(o, _):
+        chain(o, end_copy, state, ends, ends_out, ends_in, me == 0, me == n - 1)
         bt = wr_ref[o][:, :N]
         ct = wr_ref[o][:, N:]
         scores = dot(ct, bt, 1, 1)
@@ -201,11 +180,15 @@
         for h in range(heads):
             cut = slice(h * P_SIZE, (h + 1) * P_SIZE)
             decay = jnp.where(lower, jnp.exp(jnp.minimum(rc[:, h : h + 1] - rr[h : h + 1, :], 0.0)), 0.0)
-            mix = (scores * decay).astype(BF)
+            full = scores * decay
+            mix = full.astype(BF)
+            rest = (full - mix.astype(F32)).astype(BF)
             mixing[o, h] = mix
             up = (ct.astype(F32) * rising[:, h : h + 1]).astype(BF)
             outs[:, cut] = (
-                dot(mix, x_ref[o, :, cut], 1, 0) + dot(up, state[o, h].astype(BF), 1, 0)
+                dot(mix, x_ref[o, :, cut], 1, 0)
+                + dot(rest, x_ref[o, :, cut], 1, 0)
+                + dot(up, state[o, h].astype(BF), 1, 0)
             ).astype(BF)
         term = dot(scanned[o], outs[...], 0, 0)
         pf[o] = term
@@ -215,30 +198,6 @@
         return 0
 
     lax.fori_loop(0, 3, forward, 0)
-
-    for k in range(1, n):
-        w_copy(k).wait()
-        for g in range(1, n_gr):
-            g_copy(k, g).start()
-    for k in range(1, n):
-        for g in range(1, n_gr):
-            g_copy(k, g).wait()
-
-    def upstream(o, _):
-        ct = wr_ref[o][:, N:]
-        dys[o] = dot(scanned[o], wg[o], 1, 0).astype(BF)
-        rising = jnp.exp(runc[o] * scale)
-        for h in range(heads):
-            up = (ct.astype(F32) * rising[:, h : h + 1]).astype(BF)
-            grads[o, h] = dot(up, dys[o, :, h * P_SIZE : (h + 1) * P_SIZE], 0, 0).astype(BF)
-        return 0
-
-    lax.fori_loop(0, 3, upstream, 0)
-    for k in range(1, n):
-
-        @pl.when(me >= k)
-        def _():
-            grad_copy(k).start()
 
     mine_cols = pl.ds(pl.multiple_of(my_part * pcol, 128), pcol)
 
@@ -259,10 +218,43 @@
             ctx_copy(k, o).start()
         return 0
 
-    lax.fori_loop(0, 3, pair_sum, 0)
-    gather_states(gout, grads_in, grad_copy, n - 1 - me, lambda j: n - j)
+    for k in range(1, n):
+        w_copy(k).wait()
+        for g in range(1, n_gr):
+            g_copy(k, g).start()
+        if k == 1:
+            pair_sum(0, 0)
+    pair_sum(1, 0)
+    for k in range(1, n):
+        for g in range(1, n_gr):
+            g_copy(k, g).wait()
+
+    def upstream(o, _):
+        ct = wr_ref[o][:, N:]
+        dys[o] = dot(scanned[o], wg[o], 1, 0).astype(BF)
+        rising = jnp.exp(runc[o] * scale)
+        for h in range(heads):
+            up = (ct.astype(F32) * rising[:, h : h + 1]).astype(BF)
+            grads[o, h] = dot(up, dys[o, :, h * P_SIZE : (h + 1) * P_SIZE], 0, 0)
+        return 0
+
+    lax.fori_loop(0, 3, upstream, 0)
+    pair_sum(2, 0)
+
+    def dp_copy(k, o):
+        return send(cb.at[o], cb_in.at[k, o], s_c.at[k, o], r_c.at[k, o], {"dp": dp_at(k)})
+
+    def ctx_sum(o):
+        total = pf[o, pl.ds(pl.multiple_of(me * rows, rows), rows), mine_cols]
+        for k in range(1, n):
+            ctx_copy(k, o).wait()
+            total = total + sb_in[k, o].astype(F32)
+        cb[o] = total.astype(BF)
+        for k in range(1, n_dp):
+            dp_copy(k, o).start()
 
     def backward(o, _):
+        chain(o, grad_copy, gout, grads, grads_out, grads_in, me == n - 1, me == 0)
         bt = wr_ref[o][:, :N]
         ct = wr_ref[o][:, N:]
         rc = runc[o] * scale
@@ -286,6 +278,11 @@
         both = both.astype(BF)
         part[o, :, :N] = gb + dot(both, ct, 0, 0)
         part[o, :, N:] = gc + dot(both, bt, 1, 0)
+
+        @pl.when(o < 2)
+        def _():
+            ctx_sum(o)
+
         return 0
 
     lax.fori_loop(0, 3, backward, 0)
@@ -296,20 +293,7 @@
     for k in range(1, n_mp):
         mp_copy(k).start()
 
-    def dp_copy(k):
-        return send(cb, cb_in.at[k], s_c.at[k], r_c.at[k], {"dp": dp_at(k)})
-
-    def ctx_sum(o, _):
-        total = pf[o, pl.ds(pl.multiple_of(me * rows, rows), rows), mine_cols]
-        for k in range(1, n):
-            ctx_copy(k, o).wait()
-            total = total + sb_in[k, o].astype(F32)
-        cb[o] = total.astype(BF)
-        return 0
-
-    lax.fori_loop(0, 3, ctx_sum, 0)
-    for k in range(1, n_dp):
-        dp_copy(k).start()
+    ctx_sum(2)
     for k in range(1, n_mp):
         mp_copy(k).wait()
     total = part[...]
@@ -317,7 +301,8 @@
         total = total + part_in[k]
     gwr_ref[...] = total.astype(BF)
     for k in range(1, n_dp):
-        dp_copy(k).wait()
+        for o in range(3):
+            dp_copy(k, o).wait()
     for u in range(parts):
         sum_u = jnp.zeros((3, rows, pcol), F32)
         own = cb[...].astype(F32)
@@ -327,15 +312,15 @@
             sum_u = sum_u + jnp.where(belongs, piece, 0.0)
         gw_ref[:, :, u * pcol : (u + 1) * pcol] = sum_u.astype(BF)
 
-    for k in range(1, n):
-
-        @pl.when(me + k < n)
-        def _():
-            end_copy(k).wait_send()
-
-        @pl.when(me >= k)
-        def _():
-            grad_copy(k).wait_send()
+    for o in range(3):
+
+        @pl.when(me < n - 1)
+        def _():
+            end_copy(o).wait_send()
+
+        @pl.when(me > 0)
+        def _():
+            grad_copy(o).wait_send()
 
 
 def shards(sizes, head_inputs, write_read, decay_steps, scan_orders, cotangent, out_weight):
@@ -350,21 +335,21 @@
     wr = write_read.reshape(3, tokens, 2 * N)
     steps = jnp.pad(decay_steps.reshape(3, heads, tokens), ((0, 0), (0, -heads % 8), (0, 0)))
     hp = steps.shape[1]
+    chained = BF if n <= 4 else F32
     V = pltpu.VMEM
     dma = pltpu.SemaphoreType.DMA
     scratch = [
-        V((3, hp, 128), F32), V((n, 3, hp, 128), F32), V((tokens, width), BF), V((3, width, inner), BF),
-        V((3, heads, N, P_SIZE), BF), V((n, 3, heads, N, P_SIZE), BF), V((3, heads, N, P_SIZE), F32),
-        V((3, heads, N, P_SIZE), BF), V((n, 3, heads, N, P_SIZE), BF), V((3, heads, N, P_SIZE), F32),
+        V((tokens, width), BF), V((3, width, inner), BF),
+        *[V((3, heads, N, P_SIZE), kind) for kind in (F32, chained, chained, F32)] * 2,
         V((3, tokens, width), BF), V((3, heads, tokens, tokens), BF), V((tokens, inner), BF),
         V((3, tokens, inner), BF),
         V((3, width, inner), F32), V((3, width, inner), BF), V((parts, 3, width, pcol), BF),
         V((3, width, pcol), BF), V((n, 3, rows, pcol), BF), V((3, rows, pcol), BF), V((n_dp, 3, rows, pcol), BF),
         V((3, tokens, hp), F32), V((3, hp, tokens), F32),
         V((3, tokens, 2 * N), F32), V((n_mp, 3, tokens, 2 * N), F32),
-        dma((n,)), dma((n,)), dma((n,)), dma((n,)), dma((n,)), dma((n,)), dma((n, n_gr)), dma((n, n_gr)),
-        dma((n,)), dma((n,)), dma((n,)), dma((n,)), dma((parts, 3)), dma((parts, 3)), dma((n, 3)), dma((n, 3)),
-        dma((n_dp,)), dma((n_dp,)), dma((n_mp,)), dma((n_mp,)),
+        dma((n,)), dma((n,)), dma((n,)), dma((n,)), dma((n, n_gr)), dma((n, n_gr)),
+        dma((3,)), dma((3,)), dma((3,)), dma((3,)), dma((parts, 3)), dma((parts, 3)), dma((n, 3)), dma((n, 3)),
+        dma((n_dp, 3)), dma((n_dp, 3)), dma((n_mp,)), dma((n_mp,)),
     ]
     gx, gwr, gw = pl.pallas_call(
         functools.partial(kernel, sizes),

time: 188 us -> 149 us (0.79)
  Pallas kernels: 181 us -> 142 us
    pallas_call x1, Pallas kernels: 181 us -> 142 us  [shards(): pl.pallas_call(functools.partial(kernel, sizes), out_shape=(jax.ShapeDtyp...]
where the time goes in v2:
time: 149 us
  Pallas kernels  142 us (95%)
  local copies, waits for them, and re-layouts  5.39 us (4%)
    pallas_call x1, Pallas kernels, shards(): pl.pallas_call(functools.partial(kernel, sizes), out_shape=(jax.ShapeDtyp...  142 us
    unnamed x8, local copies, waits for them, and re-layouts  4.78 us

profile of v2, /device:TPU:0, one launch (start us, length us, event | category | flops | bytes accessed | tf_op | source)
XLA Modules:
  0.0 148.5 jit_solution(3027723365570401116)
XLA Ops:
  0.6 0.7 copy.13
  1.4 0.6 pad.4.steps_ref
  2.0 142.5 %shard_map.85 = (bf16[3,256,768]{2,1,0:T(8,128)(2,1)}, bf16[3,256,128]{2,1,0:T(8,128)(2,1)}, bf16[3,192,768]{2,1,0:T(8,128)(2,1)}) custom-call(bf16[3,256,768]{2,1,0:T(8,128)(2,1)} %bitcast.12, bf16[3,256,128]{2,1,0:T(8,128)(2,1)} %bitcast.15, s32[3,8,256]{2,1,0:T(8,128)} %pad.4.steps_ref, s32[2,1,256]{2,1,0:T(1,128)} %orders_ref.1, ...), custom_call_target="tpu_custom_call" | custom-call | tf_op jit(solution)/shard_map/pallas_call | solution.py:354
  144.5 0.0 copy-start.1
  144.5 0.0 copy-start
  144.5 2.4 %copy.17 = bf16[3,1,256,768]{3,2,1,0:T(8,128)(2,1)} copy(bf16[3,1,256,768]{3,2,1,0:T(8,128)(2,1)} %bitcast.13) | data formatting | bytes 2359296
  146.9 0.0 copy-done.1
  146.9 0.7 copy.18
  147.6 0.0 copy-done
  147.6 0.9 copy.19
Async XLA Ops:
  144.5 2.5 %copy-start.1 = (bf16[3,256,128]{2,1,0:T(8,128)(2,1)S(1)}, bf16[3,256,128]{2,1,0:T(8,128)(2,1)}, u32[]{:S(2)}) copy-start(bf16[3,256,128]{2,1,0:T(8,128)(2,1)} %get-tuple-element.7) | copy-start | bytes 589828
  144.5 3.1 %copy-start = (bf16[3,192,768]{2,1,0:T(8,128)(2,1)S(1)}, bf16[3,192,768]{2,1,0:T(8,128)(2,1)}, u32[]{:S(2)}) copy-start(bf16[3,192,768]{2,1,0:T(8,128)(2,1)} %get-tuple-element.17) | copy-start | bytes 2654212

commit v3 on v2

--- a/solution.py
+++ b/solution.py
@@ -98,8 +98,6 @@
 
     for k in range(1, n):
         cot_copy(k).start()
-    for k in range(1, n):
-        w_copy(k).start()
     lower = (
         lax.broadcasted_iota(jnp.int32, (tokens, tokens), 0)
         >= lax.broadcasted_iota(jnp.int32, (tokens, tokens), 1)
@@ -163,6 +161,14 @@
 
     state[...] = jnp.zeros_like(state)
     gout[...] = jnp.zeros_like(gout)
+    def chain_one(o, _):
+        chain(o, end_copy, state, ends, ends_out, ends_in, me == 0, me == n - 1)
+        return 0
+
+    lax.fori_loop(0, 3, chain_one, 0)
+
+    for k in range(1, n):
+        w_copy(k).start()
     def pair_copy(k, o):
         cols = pl.ds(pl.multiple_of((pair_at(k) - base_dp) * pcol, 128), pcol)
         return send(
@@ -170,7 +176,6 @@
         )
 
     def forward(o, _):
-        chain(o, end_copy, state, ends, ends_out, ends_in, me == 0, me == n - 1)
         bt = wr_ref[o][:, :N]
         ct = wr_ref[o][:, N:]
         scores = dot(ct, bt, 1, 1)

time: 149 us -> 138 us (0.926)
  Pallas kernels: 142 us -> 132 us
    pallas_call x1, Pallas kernels: 142 us -> 132 us  [shards(): pl.pallas_call(functools.partial(kernel, sizes), out_shape=(jax.ShapeDtyp...]
where the time goes in v3:
time: 138 us
  Pallas kernels  132 us (96%)
  local copies, waits for them, and re-layouts  5.39 us (4%)
    pallas_call x1, Pallas kernels, shards(): pl.pallas_call(functools.partial(kernel, sizes), out_shape=(jax.ShapeDtyp...  132 us
    unnamed x8, local copies, waits for them, and re-layouts  4.78 us

profile of v3, /device:TPU:0, one launch (start us, length us, event | category | flops | bytes accessed | tf_op | source)
XLA Modules:
  0.0 137.7 jit_solution(10059174650899591910)
XLA Ops:
  0.6 0.7 copy.13
  1.4 0.6 pad.4.steps_ref
  2.0 131.6 %shard_map.85 = (bf16[3,256,768]{2,1,0:T(8,128)(2,1)}, bf16[3,256,128]{2,1,0:T(8,128)(2,1)}, bf16[3,192,768]{2,1,0:T(8,128)(2,1)}) custom-call(bf16[3,256,768]{2,1,0:T(8,128)(2,1)} %bitcast.12, bf16[3,256,128]{2,1,0:T(8,128)(2,1)} %bitcast.15, s32[3,8,256]{2,1,0:T(8,128)} %pad.4.steps_ref, s32[2,1,256]{2,1,0:T(1,128)} %orders_ref.1, ...), custom_call_target="tpu_custom_call" | custom-call | tf_op jit(solution)/shard_map/pallas_call | solution.py:359
  133.6 0.0 copy-start.1
  133.6 0.0 copy-start
  133.6 2.4 %copy.17 = bf16[3,1,256,768]{3,2,1,0:T(8,128)(2,1)} copy(bf16[3,1,256,768]{3,2,1,0:T(8,128)(2,1)} %bitcast.13) | data formatting | bytes 2359296
  136.1 0.0 copy-done.1
  136.1 0.7 copy.18
  136.7 0.0 copy-done
  136.7 0.9 copy.19
Async XLA Ops:
  133.6 2.5 %copy-start.1 = (bf16[3,256,128]{2,1,0:T(8,128)(2,1)S(1)}, bf16[3,256,128]{2,1,0:T(8,128)(2,1)}, u32[]{:S(2)}) copy-start(bf16[3,256,128]{2,1,0:T(8,128)(2,1)} %get-tuple-element.7) | copy-start | bytes 589828
  133.6 3.1 %copy-start = (bf16[3,192,768]{2,1,0:T(8,128)(2,1)S(1)}, bf16[3,192,768]{2,1,0:T(8,128)(2,1)}, u32[]{:S(2)}) copy-start(bf16[3,192,768]{2,1,0:T(8,128)(2,1)} %get-tuple-element.17) | copy-start | bytes 2654212
